TPU v7x, 128 devices: a whole 4x4x4 slice. The times are simulated.
128 devices in a mesh: seq: 16 (over z_lo, y, core), rep: 8 (over z_hi, x).
Axes of the slice: x: 4, y: 4, z: 4 (z_hi: 2, z_lo: 2; z = z_hi * 2 + z_lo), core: 2. Of those that a mesh axis runs over, the one named last changes fastest.
Arguments:
- query_states: bfloat16 [8, 2048, 1024], P('rep', 'seq'), may hold values from -5 to 5
- key_states: bfloat16 [8, 2048, 1024], P('rep', 'seq'), may hold values from -5 to 5
- value_states: bfloat16 [8, 2048, 1024], P('rep', 'seq'), may hold values from -6 to 6
- grad_out: bfloat16 [8, 2048, 2048], P('rep', 'seq'), may hold values from -6 to 6
- doc_ids: int32 [8, 2048], P('rep', 'seq'), may hold values from 0 to 7, never falling along the last dimension, each value on 1 to 512 neighbouring positions
- out_weight: bfloat16 [1024, 2048], replicated, may hold values from -0.1875 to 0.1875
- owners: int32 [8], replicated, may hold values from 0 to 7, each once
- statistics: float32 [8, 2, 512, 512], P('rep', None, 'seq'), as said below
Outputs:
- query_grad: bfloat16 [8, 2048, 1024], P('rep', 'seq')
- key_grad: bfloat16 [8, 2048, 1024], P('rep', 'seq')
- value_grad: bfloat16 [8, 2048, 1024], P('rep', 'seq')
- new_statistics: float32 [8, 2, 512, 512], P('rep', None, 'seq')
- update: bfloat16 [8, 512, 512], P(None, 'seq')
Inputs may be any that keep to these rules, and one draw needn't show every extreme that they name: `doc_ids`: never falls along a sequence. `owners`: each slot holds exactly one block. `statistics`: each matrix is symmetric with a positive diagonal that dominates its row.
All inputs are finite; a program needn't handle non-finite values.
Results may differ from a plain program's by a relative error of at most 0.023.
Values may be sent and summed in bfloat16 or wider, within the bound.
No kernel may reach another device: no remote copies, remote signals or barrier semaphores. Data moves between devices by JAX's collectives and lax.ppermute only.
A program may use at most 128 MiB of HBM per device.

v0:
```python
import jax
import jax.numpy as jnp
from jax import lax
from jax.sharding import PartitionSpec as P

D = 2048
HEADS = 8
HD = 128
HW = 1024
WIN = 256
BLK = 512
NBLK = 8


masked_score = -1e30
decay_rate = 0.9
step_scale = 16.0


def passed_along(block, axis, distance):
    devices = range(lax.axis_size(axis))
    route = [(i - distance, i) for i in devices if i - distance in devices]
    return lax.ppermute(block, axis, route)


def head_major(rows_by_width):
    row_total = rows_by_width.shape[0]
    return rows_by_width.reshape(row_total, HEADS, HD).transpose(1, 0, 2)


def token_major(heads_first):
    row_total = heads_first.shape[1]
    return heads_first.transpose(1, 0, 2).reshape(row_total, HEADS * HD)


def contract_last(left_mat, right_mat):
    return lax.dot_general(
        left_mat, right_mat, (((1,), (1,)), ((), ())), preferred_element_type=jnp.float32
    )


def contract_first(left_mat, right_mat):
    return lax.dot_general(
        left_mat, right_mat, (((0,), (0,)), ((), ())), preferred_element_type=jnp.float32
    )


def highest(left_mat, right_mat):
    return jnp.dot(
        left_mat, right_mat, precision=lax.Precision.HIGHEST, preferred_element_type=jnp.float32
    )


def window_mask(query_pos, key_pos, query_doc, key_doc):
    causal = key_pos[None, :] <= query_pos[:, None]
    inside = key_pos[None, :] > query_pos[:, None] - WIN
    present = key_pos[None, :] >= 0
    same_doc = query_doc[:, None] == key_doc[None, :]
    return causal & inside & present & same_doc


def head_scores(query_head, key_head, visible):
    scores = contract_last(query_head, key_head) * HD ** (-0.5)
    return jnp.where(visible, scores, masked_score)


def forward_head(query_head, key_head, value_head, visible):
    scores = head_scores(query_head, key_head, visible)
    row_max = jnp.max(scores, axis=1, keepdims=True)
    log_norm = row_max + jnp.log(jnp.sum(jnp.exp(scores - row_max), axis=1, keepdims=True))
    weights = jnp.where(visible, jnp.exp(scores - log_norm), 0.0).astype(jnp.bfloat16)
    attended = jnp.dot(weights, value_head, preferred_element_type=jnp.float32)
    return (attended, log_norm[:, 0])


def grad_scores_head(query_head, grad_head, key_head, value_head, norm_head, dot_head, visible):
    scores = head_scores(query_head, key_head, visible)
    weights = jnp.where(visible, jnp.exp(scores - norm_head[:, None]), 0.0)
    grad_weights = contract_last(grad_head, value_head)
    grad_scores = (weights * (grad_weights - dot_head[:, None])).astype(jnp.bfloat16)
    return (grad_scores, weights.astype(jnp.bfloat16))


def inverse_root(matrix):
    identity = jnp.eye(matrix.shape[0], dtype=jnp.float32)
    frobenius = jnp.sqrt(jnp.sum(matrix * matrix))
    scaled = matrix / frobenius
    factor = (5.0 * identity - scaled) * 0.25
    square = highest(factor, factor)
    moved_mat = highest(highest(square, square), scaled)
    second = (5.0 * identity - moved_mat) * 0.25
    return highest(factor, second) * frobenius ** (-0.25)


def local(
    query_states, key_states, value_states, grad_out, doc_ids, out_weight, owners, statistics
):
    local_rows = query_states.shape[1]
    seq_index = lax.axis_index("seq")
    seq_total = lax.axis_size("seq")
    rep_total = lax.axis_size("rep")
    total_tokens = local_rows * seq_total
    query_rows = query_states[0]
    key_rows = key_states[0]
    value_rows = value_states[0]
    grad_seq = grad_out[0]
    doc_low = doc_ids[0].astype(jnp.bfloat16)
    offsets = jnp.arange(local_rows, dtype=jnp.int32)
    key_offsets = jnp.arange(3 * local_rows, dtype=jnp.int32)
    query_pos = seq_index * local_rows + offsets
    earlier = []
    for distance in (2, 1):
        earlier.append(passed_along((key_rows, value_rows, doc_low), "seq", distance))
    key_all = jnp.concatenate([earlier[0][0], earlier[1][0], key_rows], axis=0)
    value_all = jnp.concatenate([earlier[0][1], earlier[1][1], value_rows], axis=0)
    doc_all = jnp.concatenate([earlier[0][2], earlier[1][2], doc_low], axis=0)
    visible = window_mask(query_pos, (seq_index - 2) * local_rows + key_offsets, doc_low, doc_all)

    def forward_one(pieces):
        return forward_head(pieces[0], pieces[1], pieces[2], visible)

    attended_heads, norm_heads = lax.map(
        forward_one, (head_major(query_rows), head_major(key_all), head_major(value_all))
    )
    attended = token_major(attended_heads).astype(jnp.bfloat16)
    grad_attended = contract_last(grad_seq, out_weight).astype(jnp.bfloat16)
    grad_dot = jnp.sum(
        (grad_attended.astype(jnp.float32) * attended.astype(jnp.float32)).reshape(
            local_rows, HEADS, HD
        ),
        axis=2,
    )
    dot_heads = grad_dot.T
    weight_term = contract_first(attended, grad_seq) / (total_tokens * rep_total)
    row_blocks = HW // BLK
    col_blocks = D // BLK
    pick_slots = (owners[:, None] == jnp.arange(NBLK, dtype=jnp.int32)[None, :]).astype(jnp.float32)
    slot_terms = jnp.einsum(
        "ijq,ixjy->qxy",
        pick_slots.reshape(row_blocks, col_blocks, NBLK),
        weight_term.reshape(row_blocks, BLK, col_blocks, BLK),
        precision=lax.Precision.HIGHEST,
    )
    partial_sum = lax.psum_scatter(
        slot_terms.astype(jnp.bfloat16), "seq", scatter_dimension=1, tiled=True
    )
    owned = lax.psum_scatter(partial_sum, "rep", scatter_dimension=0, tiled=True).astype(
        jnp.float32
    )
    block_rows = owned.shape[1]
    grad_full, stats_full = (
        lax.all_gather(owned.astype(jnp.bfloat16), "seq", axis=1, tiled=True).astype(owned.dtype),
        lax.all_gather(statistics.astype(jnp.bfloat16), "seq", axis=2, tiled=True).astype(
            statistics.dtype
        ),
    )
    row_first = seq_index * block_rows

    def precondition(pieces):
        grad_block, old_pair = pieces
        left_stat = decay_rate * old_pair[0] + highest(grad_block, grad_block.T)
        right_stat = decay_rate * old_pair[1] + highest(grad_block.T, grad_block)
        left_root = inverse_root(left_stat)
        right_root = inverse_root(right_stat)
        own_rows = lax.dynamic_slice_in_dim(left_root, row_first, block_rows, 0)
        update_rows = highest(highest(own_rows, grad_block), right_root)
        kept_rows = jnp.stack(
            [
                lax.dynamic_slice_in_dim(left_stat, row_first, block_rows, 0),
                lax.dynamic_slice_in_dim(right_stat, row_first, block_rows, 0),
            ]
        )
        return (kept_rows, (step_scale * update_rows).astype(jnp.bfloat16))

    new_statistics, slot_updates = lax.map(precondition, (grad_full, stats_full))
    every_update = lax.all_gather(slot_updates, "rep", axis=0, tiled=True)
    pick_blocks = (owners[:, None] == jnp.arange(NBLK, dtype=jnp.int32)[None, :]).astype(
        jnp.bfloat16
    )
    update = jnp.einsum(
        "bq,qxy->bxy", pick_blocks, every_update, preferred_element_type=jnp.float32
    ).astype(jnp.bfloat16)
    head_scale = HD ** (-0.5)

    def backward_all(pieces):
        query_head, grad_head, key_head, value_head, norm_head, dot_head = pieces
        grad_scores, weights_low = grad_scores_head(
            query_head, grad_head, key_head, value_head, norm_head, dot_head, visible
        )
        head_query = jnp.dot(grad_scores, key_head, preferred_element_type=jnp.float32) * head_scale
        head_key = contract_first(grad_scores, query_head) * head_scale
        head_value = contract_first(weights_low, grad_head)
        return (head_query, head_key, head_value)

    query_heads, key_heads, value_heads = lax.map(
        backward_all,
        (
            head_major(query_rows),
            head_major(grad_attended),
            head_major(key_all),
            head_major(value_all),
            norm_heads,
            dot_heads,
        ),
    )
    key_grad_all = token_major(key_heads)
    value_grad_all = token_major(value_heads)
    key_grad = key_grad_all[2 * local_rows :]
    value_grad = value_grad_all[2 * local_rows :]
    for distance in (2, 1):
        lower = (2 - distance) * local_rows
        returned = (
            passed_along(
                key_grad_all[lower : lower + local_rows].astype(jnp.bfloat16), "seq", -distance
            ).astype(jnp.float32),
            passed_along(
                value_grad_all[lower : lower + local_rows].astype(jnp.bfloat16), "seq", -distance
            ).astype(jnp.float32),
        )
        key_grad = key_grad + returned[0]
        value_grad = value_grad + returned[1]
    query_grad = token_major(query_heads).astype(jnp.bfloat16)[None]
    return (
        query_grad,
        key_grad.astype(jnp.bfloat16)[None],
        value_grad.astype(jnp.bfloat16)[None],
        new_statistics,
        update,
    )


def solution(mesh):
    return jax.shard_map(
        local,
        mesh=mesh,
        in_specs=(
            P("rep", "seq", None),
            P("rep", "seq", None),
            P("rep", "seq", None),
            P("rep", "seq", None),
            P("rep", "seq"),
            P(),
            P(),
            P("rep", None, "seq", None),
        ),
        out_specs=(
            P("rep", "seq", None),
            P("rep", "seq", None),
            P("rep", "seq", None),
            P("rep", None, "seq", None),
            P(None, "seq", None),
        ),
        check_vma=False,
    )
```

profile of v0, /device:TPU:0, one launch (start us, length us, event | category | flops | bytes accessed | tf_op | source)
XLA Modules:
  0.0 342.5 jit_solution(3265333775818206123)
XLA Ops:
  7.2 1.2 copy.49
  8.4 1.3 collective-permute-start.1
  9.7 4.2 %collective-permute-start = (bf16[128,1024]{0,1:T(8,128)(2,1)S(1)}, bf16[128,1024]{0,1:T(8,128)(2,1)S(1)}, u32[]{:S(2)}, u32[]{:S(2)}) collective-permute-start(bf16[128,1024]{0,1:T(8,128)(2,1)S(1)} %bitcast.251), channel_id=1, source_target_pairs={{0,16},{8,24},{16,32},{24,40},{32,48},{40,56},{48,64},{56,72},{64,... | collective-permute-start | bytes 786440 | tf_op jit(solution)/shard_map/ppermute | solution.py:23
  13.9 1.1 copy.51
  15.0 3.3 collective-permute-start.5
  18.4 3.9 %collective-permute-start.4 = (bf16[128,1024]{0,1:T(8,128)(2,1)S(1)}, bf16[128,1024]{0,1:T(8,128)(2,1)}, u32[]{:S(2)}, u32[]{:S(2)}) collective-permute-start(bf16[128,1024]{0,1:T(8,128)(2,1)S(1)} %bitcast.248), channel_id=1, source_target_pairs={{0,16},{8,24},{16,32},{24,40},{32,48},{40,56},{48,64},{56,72},{64,... | collective-permute-start | bytes 786440 | tf_op jit(solution)/shard_map/ppermute | solution.py:23
  22.9 1.9 collective-permute-start.3
  24.9 1.1 copy.48
  26.0 7.7 %collective-permute-start.2 = (bf16[128]{0:T(256)(128)(2,1)S(1)}, bf16[128]{0:T(256)(128)(2,1)S(1)}, u32[]{:S(2)}, u32[]{:S(2)}) collective-permute-start(bf16[128]{0:T(256)(128)(2,1)S(1)} %convert_bitcast_fusion.2), channel_id=1, source_target_pairs={{0,16},{8,24},{16,32},{24,40},{32,48},{40,56},{48,64},{56,72},{64,... | collective-permute-start | bytes 776 | tf_op jit(solution)/shard_map/ppermute | solution.py:23
  34.0 1.0 collective-permute-done.2
  35.5 1.1 maximum_bitcast_fusion.1
  37.0 6.6 %while.33 = (s32[]{:T(128)}, bf16[8,128,128]{2,1,0:T(8,128)(2,1)S(1)}, f32[8,128]{1,0:T(8,128)S(1)}, bf16[8,128,128]{2,1,0:T(8,128)(2,1)S(1)}, bf16[8,384,128]{2...) while((s32[]{:T(128)}, ...), condition=%wide.region_3.4_spmd.clone, body=%wide.region_0.3_spmd.clone.sunk | while | flops 26345344 | bytes 901777 | solution.py:122
  43.7 4.5 %convolution_multiply_fusion.4 = f32[1024,2048]{1,0:T(8,128)} fusion(bf16[1,128,2048]{2,1,0:T(8,128)(2,1)S(1)} %copy-done, bf16[8,128,128]{2,1,0:T(8,128)(2,1)S(1)} %get-tuple-element.121), kind=kOutput, calls=%fused_computation.62 | convolution fusion | flops 538968064 | bytes 9175040 | tf_op jit(solution)/shard_map/dot_general | solution.py:43
  48.2 10.9 %reshape.147 = f32[2,512,4,512]{3,2,1,0:T(4,128)} reshape(f32[1024,2048]{1,0:T(8,128)} %convolution_multiply_fusion.4) | data formatting | bytes 16777216 | tf_op jit(solution)/shard_map/reshape | solution.py:141
  59.1 9.8 %bitcast_convert_fusion = bf16[8,512,512]{2,0,1:T(8,128)(2,1)} fusion(f32[2,512,4,512]{3,2,1,0:T(4,128)} %reshape.147, s32[2,4]{1,0:T(2,128)S(1)} %eq.71), kind=kOutput, calls=%fused_computation.61 | convolution fusion | flops 203423808 | bytes 12582944 | tf_op jit(solution)/shard_map/ijq,ixjy->qxy/dot_general | solution.py:138
  70.5 3.7 %convolution_convert_fusion.1 = bf16[128,1024]{1,0:T(8,128)(2,1)S(1)} fusion(bf16[1024,2048]{1,0:T(8,128)(2,1)} %param.17, bf16[1,128,2048]{2,1,0:T(8,128)(2,1)S(1)} %copy-done), kind=kOutput, calls=%fused_computation.73 | convolution fusion | flops 537001984 | bytes 4980736 | tf_op jit(solution)/shard_map/dot_general | solution.py:37
  75.4 39.5 %while.34 = (s32[]{:T(128)}, bf16[8,128,128]{2,1,0:T(8,128)(2,1)S(1)}, f32[8,384,128]{2,1,0:T(8,128)S(1)}, f32[8,384,128]{2,1,0:T(8,128)}, bf16[8,128,128]{2,1,0...) while((s32[]{:T(128)}, ...), condition=%wide.region_6.7_spmd.clone, body=%wide.region_5.6_spmd.clone.sunk | while | flops 63766528 | bytes 1782953 | solution.py:195
  75.4 1.0 fusion.164
  76.4 1.1 fusion.165
  77.7 1.0 fusion.167
  78.7 1.7 fusion.168
  81.4 1.1 fusion.165
  82.7 1.0 fusion.167
  83.7 1.7 fusion.168
  86.3 1.1 fusion.165
  87.6 1.0 fusion.167
  88.6 1.7 fusion.168
  91.2 1.1 fusion.165
  93.5 1.7 fusion.168
  96.1 1.1 fusion.165
  97.5 1.0 fusion.167
  98.4 1.7 fusion.168
  101.1 1.1 fusion.165
  102.4 1.0 fusion.167
  103.4 1.7 fusion.168
  106.0 1.1 fusion.165
  107.3 1.0 fusion.167
  108.3 1.6 fusion.168
  110.9 1.1 fusion.165
  113.2 1.7 fusion.168
  116.4 1.3 collective-permute-start.7
  118.4 1.3 collective-permute-start.6
  119.9 20.7 %reduce-scatter.3.cloned.1.call-done = bf16[8,32,512]{2,0,1:T(8,128)(2,1)} async-done(((bf16[8,512,512]{2,0,1:T(8,128)(2,1)}), bf16[8,32,512]{2,0,1:T(8,128)(2,1)}) %reduce-scatter.3.cloned.1.call-update) | async-done | bytes 262160 | tf_op jit(solution)/shard_map/reduce_scatter | solution.py:144
  140.5 1.8 copy.70
  143.1 1.3 collective-permute-start.9
  145.2 1.3 collective-permute-start.8
  147.5 1.7 fusion.86
  149.3 7.8 %collective-permute-done.8 = bf16[128,1024]{1,0:T(8,128)(2,1)S(1)} collective-permute-done((bf16[128,1024]{1,0:T(8,128)(2,1)}, bf16[128,1024]{1,0:T(8,128)(2,1)S(1)}, u32[]{:S(2)}, u32[]{:S(2)}) %collective-permute-start.8) | collective-permute-done | bytes 262176 | tf_op jit(solution)/shard_map/ppermute | solution.py:23
  157.0 1.8 fusion.87
  158.9 19.7 %all-gather.3.cloned.1.call-done = bf16[1,2,512,512]{3,2,1,0:T(8,128)(2,1)} async-done(((bf16[1,2,32,512]{3,2,1,0:T(8,128)(2,1)}), bf16[1,2,512,512]{3,2,1,0:T(8,128)(2,1)}) %all-gather.3.cloned.1.call-update) | async-done | bytes 1048592 | tf_op jit(solution)/shard_map/all_gather | solution.py:153
  178.6 1.5 convert_element_type.137
  180.1 74.1 %reduce-scatter.5.cloned.1.call-done = bf16[1,32,512]{2,1,0:T(8,128)(2,1)} async-done(((bf16[8,32,512]{2,1,0:T(8,128)(2,1)}), bf16[1,32,512]{2,1,0:T(8,128)(2,1)}) %reduce-scatter.5.cloned.1.call-update) | async-done | bytes 32784 | tf_op jit(solution)/shard_map/reduce_scatter | solution.py:147
  254.2 20.7 %all_gather.10 = bf16[1,512,512]{2,1,0:T(8,128)(2,1)S(1)} all-gather(bf16[1,32,512]{2,1,0:T(8,128)(2,1)} %reduce-scatter.5.cloned.1.call-done), channel_id=1, replica_groups=mesh['seq'=16,'rep'=8] {'seq'}, dimensions={1}, use_global_device_ids=true | all-gather | bytes 557056 | tf_op jit(solution)/shard_map/all_gather | solution.py:152
  274.9 1.2 multiply_reduce_fusion
  276.1 1.2 multiply_reduce_fusion.1
  279.0 3.6 %fusion.62 = f32[512,512]{1,0:T(8,128)S(1)} fusion(f32[512,512]{1,0:T(8,128)} %copy-done.5, f32[]{:T(128)S(6)} %sqrt.8), kind=kOutput, calls=%fused_computation.87 | convolution fusion | flops 1611923456 | bytes 2097156 | tf_op jit(solution)/shard_map/while/body/eval_jaxpr/dot_general | solution.py:49
  283.4 3.6 %fusion.58 = f32[512,512]{1,0:T(8,128)S(1)} fusion(f32[512,512]{1,0:T(8,128)} %copy-done.3, f32[]{:T(128)S(6)} %sqrt.9), kind=kOutput, calls=%fused_computation.85 | convolution fusion | flops 1611923456 | bytes 2097156 | tf_op jit(solution)/shard_map/while/body/eval_jaxpr/dot_general | solution.py:49
  287.1 1.8 fusion.112
  288.9 1.9 fusion.50
  290.8 2.0 fusion.60
  292.8 1.8 fusion.113
  294.6 2.1 fusion.51
  297.1 2.0 convolution_multiply_fusion.5
  299.8 34.4 %all-gather = bf16[256,512]{1,0:T(8,128)(2,1)S(1)} all-gather(bf16[32,512]{1,0:T(8,128)(2,1)S(1)} %fusion.52), channel_id=2, replica_groups=mesh['seq'=16,'rep'=8] {'rep'}, dimensions={0}, use_global_device_ids=true | all-gather | bytes 294912 | tf_op jit(solution)/shard_map/all_gather | solution.py:176
  (141 shorter events, 30.1 us)
Async XLA Ops:
  7.2 36.5 %copy-start = (bf16[1,128,2048]{2,1,0:T(8,128)(2,1)S(1)}, bf16[1,128,2048]{2,1,0:T(8,128)(2,1)}, u32[]{:S(2)}) copy-start(bf16[1,128,2048]{2,1,0:T(8,128)(2,1)} %param.15) | copy-start | bytes 1572868
  7.2 26.7 %copy-start.11 = (s32[8]{0:T(128)S(1)}, s32[8]{0:T(128)}, u32[]{:S(2)}) copy-start(s32[8]{0:T(128)} %param.18) | copy-start | bytes 100
  7.2 133.3 %reduce-scatter.3.cloned.1.call-start = ((), (), s32[]{:S(2)}) async-start(), calls=%async_computation.3 | async-start | bytes 4456448 | tf_op jit(solution)/shard_map/reduce_scatter | solution.py:144
  8.4 26.6 %collective-permute-start.1 = (bf16[128,1024]{0,1:T(8,128)(2,1)S(1)}, bf16[128,1024]{0,1:T(8,128)(2,1)S(1)}, u32[]{:S(2)}, u32[]{:S(2)}) collective-permute-start(bf16[128,1024]{0,1:T(8,128)(2,1)S(1)} %bitcast.250), channel_id=1, source_target_pairs={{0,8},{8,16},{16,24},{24,32},{32,40},{40,48},{48,56},{56,64},{64,7... | collective-permute-start | bytes 786440 | tf_op jit(solution)/shard_map/ppermute | solution.py:23
  9.7 25.3 %collective-permute-start = (bf16[128,1024]{0,1:T(8,128)(2,1)S(1)}, bf16[128,1024]{0,1:T(8,128)(2,1)S(1)}, u32[]{:S(2)}, u32[]{:S(2)}) collective-permute-start(bf16[128,1024]{0,1:T(8,128)(2,1)S(1)} %bitcast.251), channel_id=1, source_target_pairs={{0,16},{8,24},{16,32},{24,40},{32,48},{40,56},{48,64},{56,72},{64,... | collective-permute-start | bytes 786440 | tf_op jit(solution)/shard_map/ppermute | solution.py:23
  15.0 20.4 %collective-permute-start.5 = (bf16[128,1024]{0,1:T(8,128)(2,1)S(1)}, bf16[128,1024]{0,1:T(8,128)(2,1)S(1)}, u32[]{:S(2)}, u32[]{:S(2)}) collective-permute-start(bf16[128,1024]{0,1:T(8,128)(2,1)S(1)} %bitcast.247), channel_id=1, source_target_pairs={{0,8},{8,16},{16,24},{24,32},{32,40},{40,48},{48,56},{56,64},{64,7... | collective-permute-start | bytes 786440 | tf_op jit(solution)/shard_map/ppermute | solution.py:23
  18.4 17.1 %collective-permute-start.4 = (bf16[128,1024]{0,1:T(8,128)(2,1)S(1)}, bf16[128,1024]{0,1:T(8,128)(2,1)}, u32[]{:S(2)}, u32[]{:S(2)}) collective-permute-start(bf16[128,1024]{0,1:T(8,128)(2,1)S(1)} %bitcast.248), channel_id=1, source_target_pairs={{0,16},{8,24},{16,32},{24,40},{32,48},{40,56},{48,64},{56,72},{64,... | collective-permute-start | bytes 786440 | tf_op jit(solution)/shard_map/ppermute | solution.py:23
  22.9 3.1 collective-permute-start.3
  26.0 9.0 %collective-permute-start.2 = (bf16[128]{0:T(256)(128)(2,1)S(1)}, bf16[128]{0:T(256)(128)(2,1)S(1)}, u32[]{:S(2)}, u32[]{:S(2)}) collective-permute-start(bf16[128]{0:T(256)(128)(2,1)S(1)} %convert_bitcast_fusion.2), channel_id=1, source_target_pairs={{0,16},{8,24},{16,32},{24,40},{32,48},{40,56},{48,64},{56,72},{64,... | collective-permute-start | bytes 776 | tf_op jit(solution)/shard_map/ppermute | solution.py:23
  43.6 4.5 %copy-start.2 = (bf16[8,384,128]{2,1,0:T(8,128)(2,1)}, bf16[8,384,128]{2,1,0:T(8,128)(2,1)S(1)}, u32[]{:S(2)}) copy-start(bf16[8,384,128]{2,1,0:T(8,128)(2,1)S(1)} %get-tuple-element.615) | copy-start | bytes 2359300
  43.6 4.5 %copy-start.9 = (bf16[8,128,128]{2,1,0:T(8,128)(2,1)}, bf16[8,128,128]{2,1,0:T(8,128)(2,1)S(1)}, u32[]{:S(2)}) copy-start(bf16[8,128,128]{2,1,0:T(8,128)(2,1)S(1)} %get-tuple-element.623) | copy-start | bytes 786436
  68.8 0.9 copy-start.10
  68.8 109.7 %all-gather.3.cloned.1.call-start = ((), (), s32[]{:S(2)}) async-start(), calls=%async_computation.2 | async-start | bytes 1114112 | tf_op jit(solution)/shard_map/all_gather | solution.py:153
  70.4 183.8 %reduce-scatter.5.cloned.1.call-start = ((), (), s32[]{:S(2)}) async-start(), calls=%async_computation.4 | async-start | bytes 294912 | tf_op jit(solution)/shard_map/reduce_scatter | solution.py:147
  114.9 0.7 copy-start.7
  115.0 4.7 %copy-start.1 = (f32[8,384,128]{2,1,0:T(8,128)S(1)}, f32[8,384,128]{2,1,0:T(8,128)}, u32[]{:S(2)}) copy-start(f32[8,384,128]{2,1,0:T(8,128)} %get-tuple-element.124) | copy-start | bytes 4718596
  116.4 31.1 %collective-permute-start.7 = (bf16[128,1024]{1,0:T(8,128)(2,1)}, bf16[128,1024]{1,0:T(8,128)(2,1)S(1)}, u32[]{:S(2)}, u32[]{:S(2)}) collective-permute-start(bf16[128,1024]{1,0:T(8,128)(2,1)} %bitcast.203), channel_id=1, source_target_pairs={{8,0},{16,8},{24,16},{32,24},{40,32},{48,40},{56,48},{64,56},{72,6... | collective-permute-start | bytes 786440 | tf_op jit(solution)/shard_map/ppermute | solution.py:23
  118.4 29.1 %collective-permute-start.6 = (bf16[128,1024]{1,0:T(8,128)(2,1)}, bf16[128,1024]{1,0:T(8,128)(2,1)}, u32[]{:S(2)}, u32[]{:S(2)}) collective-permute-start(bf16[128,1024]{1,0:T(8,128)(2,1)} %bitcast.204), channel_id=1, source_target_pairs={{16,0},{24,8},{32,16},{40,24},{48,32},{56,40},{64,48},{72,56},{80,... | collective-permute-start | bytes 786440 | tf_op jit(solution)/shard_map/ppermute | solution.py:23
  119.9 26.6 %copy-start.8 = (bf16[8,128,128]{2,1,0:T(8,128)(2,1)S(1)}, bf16[8,128,128]{2,1,0:T(8,128)(2,1)}, u32[]{:S(2)}) copy-start(bf16[8,128,128]{2,1,0:T(8,128)(2,1)} %copy-done.7) | copy-start | bytes 786436
  143.1 6.1 %collective-permute-start.9 = (bf16[128,1024]{1,0:T(8,128)(2,1)}, bf16[128,1024]{1,0:T(8,128)(2,1)S(1)}, u32[]{:S(2)}, u32[]{:S(2)}) collective-permute-start(bf16[128,1024]{1,0:T(8,128)(2,1)} %bitcast.201), channel_id=1, source_target_pairs={{8,0},{16,8},{24,16},{32,24},{40,32},{48,40},{56,48},{64,56},{72,6... | collective-permute-start | bytes 786440 | tf_op jit(solution)/shard_map/ppermute | solution.py:23
  145.2 11.8 %collective-permute-start.8 = (bf16[128,1024]{1,0:T(8,128)(2,1)}, bf16[128,1024]{1,0:T(8,128)(2,1)S(1)}, u32[]{:S(2)}, u32[]{:S(2)}) collective-permute-start(bf16[128,1024]{1,0:T(8,128)(2,1)} %bitcast.202), channel_id=1, source_target_pairs={{16,0},{24,8},{32,16},{40,24},{48,32},{56,40},{64,48},{72,56},{80,... | collective-permute-start | bytes 786440 | tf_op jit(solution)/shard_map/ppermute | solution.py:23
  276.1 1.2 copy-start.3
  277.3 1.0 copy-start.5
  287.1 1.9 copy-start.6
  292.8 1.9 copy-start.4
Sparse Core Ops, SparseCore 0:
  69.0 71.5 reduce-scatter.2
  142.8 35.7 all-gather.2
  182.1 71.9 reduce-scatter.4
where the time goes:
time: 345 us; the launch traced here: 342 us
  waiting for transfers between devices  123 us (36%)
  matrix products  84.2 us (24%)
  blocking collectives  55.1 us (16%)
  starting transfers between devices  27.5 us (8%)
  local copies, waits for them, and re-layouts  25.7 us (7%)
  between operations  15.8 us (5%)
  other arithmetic  10.3 us (3%)
    reduce_scatter x1, waiting for transfers between devices, local(): lax.psum_scatter(partial_sum, 'rep', scatter_dimension=0, tiled=True)  74.1 us
    all_gather x1, blocking collectives, local(): every_update = lax.all_gather(slot_updates, 'rep', axis=0, tiled=True)  34.4 us
    ppermute x10, starting transfers between devices, passed_along(): return lax.ppermute(block, axis, route)  27.4 us
    dot_general x17, matrix products, contract_first(): lax.dot_general(left_mat, right_mat, (((0,), (0,)), ((), ())), preferred_...  25.6 us
    dot_general x25, matrix products, contract_last(): lax.dot_general(left_mat, right_mat, (((1,), (1,)), ((), ())), preferred_...  22.6 us
    dot_general x12, matrix products, highest(): jnp.dot(left_mat, right_mat, precision=lax.Precision.HIGHEST, preferred_e...  22.3 us
    all_gather x1, blocking collectives, local(): lax.all_gather(owned.astype(jnp.bfloat16), 'seq', axis=1, tiled=True)  20.7 us
    reduce_scatter x1, waiting for transfers between devices, local(): lax.psum_scatter(slot_terms.astype(jnp.bfloat16), 'seq', scatter_dimensio...  20.7 us
  transfers between devices with their start and end apart: 13, of which 5 were waited for; matrix products, arithmetic and copies ran while one was open for 17% of the time, Pallas kernels for 0%

commit v1 on v0

v1 whole, which is shorter than its diff:
```python
import functools

import jax
import jax.numpy as jnp
from jax import lax
from jax.experimental import pallas as pl
from jax.experimental.pallas import tpu as pltpu
from jax.sharding import Mesh, PartitionSpec as P

D = 2048
HD = 128
HW = 1024
TOK = 128
BLK = 512
NBLK = 8
HALF = HW // 2
PAIR = 2 * TOK
QTR = 256
KVW = 2 * HALF + TOK

SEQ = ("zl", "y", "c")
REP = ("zh", "x")
OUTER = ("zl", "zh", "x")
N_SEQ = 16
N_OUTER = 16
ROWS = BLK // N_SEQ
PART = 128

masked_score = -1e30
decay_rate = 0.9
step_scale = 16.0
head_scale = HD ** (-0.5)
weight_scale = 1.0 / 16384.0

f32 = jnp.float32
bf16 = jnp.bfloat16
VMEM_LIMIT = 48 * 1024 * 1024
WHOLE = pl.BlockSpec(memory_space=pltpu.VMEM)
SCALARS = pl.BlockSpec(memory_space=pltpu.SMEM)


def nt(left, right):
    return lax.dot_general(left, right, (((1,), (1,)), ((), ())), preferred_element_type=f32)


def tn(left, right):
    return lax.dot_general(left, right, (((0,), (0,)), ((), ())), preferred_element_type=f32)


def nn(left, right):
    return lax.dot_general(left, right, (((1,), (0,)), ((), ())), preferred_element_type=f32)


def call(body, outs, args, scratch=(), flops=0, nbytes=0, name=None):
    specs = [SCALARS if a.dtype == jnp.int32 and a.ndim == 1 else WHOLE for a in args]
    return pl.pallas_call(
        body,
        out_shape=outs,
        in_specs=specs,
        out_specs=jax.tree.map(lambda _: WHOLE, outs),
        scratch_shapes=list(scratch),
        compiler_params=pltpu.CompilerParams(vmem_limit_bytes=VMEM_LIMIT),
        cost_estimate=pl.CostEstimate(flops=flops, bytes_accessed=nbytes, transcendentals=0),
        name=name,
    )(*args)


def shaped(shape, dtype):
    return jax.ShapeDtypeStruct(shape, dtype)


def pick(core, ref, half):
    first = ref[:, half * HALF : half * HALF + QTR]
    second = ref[:, half * HALF + QTR : (half + 1) * HALF]
    return jnp.where(core == 0, first, second)


def pack_kernel(at_ref, key_ref, value_ref, doc_ref, own_ref, other_ref):
    core = at_ref[0]
    docs = jnp.broadcast_to(doc_ref[...].astype(f32), (TOK, TOK)).T.astype(bf16)
    for out_ref, which in ((own_ref, core), (other_ref, 1 - core)):
        for half in range(2):
            out_ref[:, half * QTR : (half + 1) * QTR] = pick(which, key_ref, half)
            out_ref[:, HALF + half * QTR : HALF + (half + 1) * QTR] = pick(which, value_ref, half)
        out_ref[:, 2 * HALF :] = docs


def own_rows(core):
    return pl.ds(pl.multiple_of(core * TOK, TOK), TOK)


def grad_attended_kernel(
    at_ref, query_ref, query_other_ref, grad_ref, grad_other_ref, weight_ref,
    attended_grad_ref, query_all_ref, grad_all_ref,
):
    core = at_ref[0]
    mine, other = own_rows(core), own_rows(1 - core)
    for half in range(2):
        cols = slice(half * QTR, (half + 1) * QTR)
        query_all_ref[mine, cols] = pick(core, query_ref, half)
        query_all_ref[other, cols] = pick(core, query_other_ref, half)
    grad_all_ref[mine, :] = grad_ref[...]
    grad_all_ref[other, :] = grad_other_ref[...]
    grad_rows = grad_all_ref[...]
    for half in range(2):
        start = pl.multiple_of(half * HALF + core * QTR, QTR)
        weight_rows = weight_ref[pl.ds(start, QTR), :]
        attended_grad_ref[:, half * QTR : (half + 1) * QTR] = nt(grad_rows, weight_rows).astype(bf16)


def place_blocks(core, own_ref, other_ref, before_ref, crossed_ref, all_ref):
    for ref, place in (
        (before_ref, core), (crossed_ref, 1 - core), (own_ref, 2 + core), (other_ref, 3 - core)
    ):
        all_ref[pl.ds(pl.multiple_of(place * TOK, TOK), TOK), :] = ref[...]


def forward_kernel(
    at_ref, owner_ref, query_ref, grad_ref, own_ref, other_ref, before_ref, crossed_ref,
    terms_ref, weights_ref, all_ref, attended_ref,
):
    core, chip = at_ref[0], at_ref[1]
    place_blocks(core, own_ref, other_ref, before_ref, crossed_ref, all_ref)
    doc_cols = [all_ref[b * TOK : (b + 1) * TOK, 2 * HALF :].astype(f32) for b in range(4)]
    doc_row = jnp.concatenate([block.T for block in doc_cols], axis=1)
    query_at = lax.broadcasted_iota(jnp.int32, (TOK, 3 * TOK), 0)
    key_at = lax.broadcasted_iota(jnp.int32, (TOK, 3 * TOK), 1)
    window = (key_at <= query_at + PAIR) & (key_at > query_at)
    for part in range(2):
        same = jnp.concatenate([doc_cols[2 + part]] * 3, axis=1) == doc_row[:, part * TOK : (part + 3) * TOK]
        present = key_at + part * TOK >= jnp.where(chip > 0, 0, PAIR)
        visible = window & same & present
        rows = slice(part * TOK, (part + 1) * TOK)
        keys = slice(part * TOK, (part + 3) * TOK)
        for head in range(4):
            cols = slice(head * HD, (head + 1) * HD)
            value_cols = slice(HALF + head * HD, HALF + (head + 1) * HD)
            scores = nt(query_ref[rows, cols], all_ref[keys, cols]) * head_scale
            scores = jnp.where(visible, scores, masked_score)
            row_max = jnp.max(scores, axis=1, keepdims=True)
            grown = jnp.exp(scores - row_max)
            total = jnp.sum(grown, axis=1, keepdims=True)
            weights = (grown * (1.0 / total)).astype(bf16)
            weights_ref[head, part] = weights
            attended_ref[rows, cols] = nn(weights, all_ref[keys, value_cols]).astype(bf16)
    for i in range(2):
        turned = attended_ref[:, i * QTR : (i + 1) * QTR].astype(f32).T.astype(bf16)
        for j in range(4):
            slot = owner_ref[4 * i + j]
            term = (nn(turned, grad_ref[:, j * BLK : (j + 1) * BLK]) * weight_scale).astype(bf16)
            terms_ref[0, slot] = term[:PART]
            terms_ref[1, slot] = term[PART:]


def backward_kernel(
    at_ref, weights_ref, query_ref, grad_ref, own_ref, other_ref, before_ref, crossed_ref,
    query_out_ref, sent_ref, kept_ref, all_ref, sum_ref,
):
    core = at_ref[0]
    place_blocks(core, own_ref, other_ref, before_ref, crossed_ref, all_ref)
    sum_ref[...] = jnp.zeros_like(sum_ref)
    for part in range(2):
        rows = slice(part * TOK, (part + 1) * TOK)
        keys = slice(part * TOK, (part + 3) * TOK)
        for head in range(4):
            cols = slice(head * HD, (head + 1) * HD)
            value_cols = slice(HALF + head * HD, HALF + (head + 1) * HD)
            low = weights_ref[head, part]
            weights = low.astype(f32)
            grad_head = grad_ref[rows, cols]
            query_head = query_ref[rows, cols]
            grad_weights = nt(grad_head, all_ref[keys, value_cols])
            grad_dot = jnp.sum(weights * grad_weights, axis=1, keepdims=True)
            grad_scores = (weights * (grad_weights - grad_dot)).astype(bf16)
            query_out_ref[rows, cols] = (nn(grad_scores, all_ref[keys, cols]) * head_scale).astype(bf16)
            sum_ref[keys, cols] += tn(grad_scores, query_head) * head_scale
            sum_ref[keys, value_cols] += tn(low, grad_head)
    sent_ref[...] = sum_ref[:PAIR].astype(bf16)
    kept_ref[...] = sum_ref[PAIR:]


def gather_grads_kernel(at_ref, query_ref, kept_ref, back_ref, mine_ref, other_ref):
    core = at_ref[0]
    for out_ref, rows in ((mine_ref, own_rows(core)), (other_ref, own_rows(1 - core))):
        out_ref[:, :HALF] = query_ref[rows, :]
        out_ref[:, HALF:] = (kept_ref[rows, :] + back_ref[rows, :].astype(f32)).astype(bf16)


def whole_width_kernel(at_ref, mine_ref, other_ref, query_ref, key_ref, value_ref):
    core = at_ref[0]
    for n, out_ref in enumerate((query_ref, key_ref, value_ref)):
        for half in range(2):
            cols = slice(n * HALF + half * QTR, n * HALF + (half + 1) * QTR)
            mine, other = mine_ref[:, cols], other_ref[:, cols]
            out_ref[0, :, half * HALF : half * HALF + QTR] = jnp.where(core == 0, mine, other)
            out_ref[0, :, half * HALF + QTR : (half + 1) * HALF] = jnp.where(core == 0, other, mine)


def sum_parts_kernel(parts_ref, total_ref):
    total = parts_ref[0].astype(f32)
    for n in range(1, N_OUTER):
        total = total + parts_ref[n].astype(f32)
    total_ref[...] = total.astype(bf16)


def newton_kernel(
    at_ref, grad_ref, grad_zl_ref, grad_c_ref, grad_zl_c_ref, stats_ref, stat_rows_ref,
    new_rows_ref, update_ref, slot_ref, left_ref, right_ref,
):
    core, low, row_first = at_ref[0], at_ref[2], at_ref[3]
    for ref, c, zl in (
        (grad_ref, core, low), (grad_zl_ref, core, 1 - low),
        (grad_c_ref, 1 - core, low), (grad_zl_c_ref, 1 - core, 1 - low),
    ):
        slot_ref[pl.ds(pl.multiple_of((2 * c + zl) * PART, PART), PART), :] = ref[...]
    slot = slot_ref[...]
    own = pl.ds(pl.multiple_of(row_first, ROWS), ROWS)
    left_ref[...] = nt(slot, slot)
    right_ref[...] = tn(slot, slot)
    new_rows_ref[0, 0] = decay_rate * stat_rows_ref[0, 0] + left_ref[own, :]
    new_rows_ref[0, 1] = decay_rate * stat_rows_ref[0, 1] + right_ref[own, :]
    left = decay_rate * stats_ref[:, 0].reshape(BLK, BLK).astype(f32) + left_ref[...]
    right = decay_rate * stats_ref[:, 1].reshape(BLK, BLK).astype(f32) + right_ref[...]

    def scaled(stat):
        norm_square = jnp.sum(jnp.sum(stat * stat, axis=0, keepdims=True), axis=1, keepdims=True)
        matrix = stat * lax.rsqrt(norm_square)
        low_matrix = matrix.astype(bf16)
        step = (nn(low_matrix, low_matrix) - 10.0 * matrix).astype(bf16)
        return matrix, low_matrix, step, jnp.exp(-0.125 * jnp.log(norm_square))

    left_matrix, left_low, left_step, left_scale = scaled(left)
    right_matrix, right_low, right_step, right_scale = scaled(right)
    left_ref[...] = left_matrix
    identity_rows = jnp.where(
        lax.broadcasted_iota(jnp.int32, (ROWS, BLK), 0) + row_first
        == lax.broadcasted_iota(jnp.int32, (ROWS, BLK), 1),
        1.0,
        0.0,
    )

    def rooted(factor, low_matrix, step):
        square = (25.0 * factor + nn(factor.astype(bf16), step)) * 0.0625
        fourth = (25.0 * square + nn(square.astype(bf16), step)) * 0.0625
        return (5.0 * factor - nn(fourth.astype(bf16), low_matrix)) * 0.25

    left_factor = (5.0 * identity_rows - left_ref[own, :]) * 0.25
    left_rows = rooted(left_factor, left_low, left_step)
    moved = nn(left_rows.astype(bf16), slot)
    right_factor = (5.0 * moved - nn(moved.astype(bf16), right_low)) * 0.25
    update = rooted(right_factor, right_low, right_step) * (step_scale * left_scale * right_scale)
    update_low = update.astype(bf16)
    for n in range(NBLK):
        update_ref[n] = update_low


def order_kernel(owner_ref, slots_ref, blocks_ref):
    for block in range(NBLK):
        blocks_ref[block] = slots_ref[owner_ref[block]]


def swapped(block, axis, mask=1):
    n = lax.axis_size(axis)
    return lax.ppermute(block, axis, [(i, i ^ mask) for i in range(n)])


def local(query_states, key_states, value_states, grad_out, doc_ids, out_weight, owners, statistics):
    core, low, along = lax.axis_index("c"), lax.axis_index("zl"), lax.axis_index("y")
    chip = low * 4 + along
    at = jnp.stack([core, chip, low, (chip * 2 + core) * ROWS]).astype(jnp.int32)
    query, key, value, grad = query_states[0], key_states[0], value_states[0], grad_out[0]

    stats_all = lax.all_gather(statistics[0].astype(bf16), SEQ, axis=0, tiled=False)

    own, other = call(
        pack_kernel,
        (shaped((TOK, KVW), bf16), shaped((TOK, KVW), bf16)),
        (at, key, value, doc_ids),
        name="pack",
    )
    before = lax.ppermute(own, SEQ, [(i, i + 2) for i in range(N_SEQ - 2)])
    crossed = lax.ppermute(other, SEQ, [(i, (i ^ 1) + 2) for i in range(N_SEQ - 2)])
    partner = swapped(other, "c")
    query_partner = swapped(query, "c")
    grad_partner = swapped(grad, "c")

    attended_grad, query_all, grad_all = call(
        grad_attended_kernel,
        (shaped((PAIR, HALF), bf16), shaped((PAIR, HALF), bf16), shaped((PAIR, D), bf16)),
        (at, query, query_partner, grad, grad_partner, out_weight),
        flops=2 * PAIR * HALF * D,
        nbytes=8 * 2**20,
        name="grad_attended",
    )
    terms, weights = call(
        forward_kernel,
        (shaped((2, NBLK, PART, BLK), bf16), shaped((4, 2, TOK, 3 * TOK), bf16)),
        (at, owners, query_all, grad_all, own, partner, before, crossed),
        scratch=(pltpu.VMEM((2 * PAIR, KVW), bf16), pltpu.VMEM((PAIR, HALF), bf16)),
        flops=2 * PAIR * HALF * (D + 6 * TOK),
        nbytes=6 * 2**20,
        name="forward",
    )
    parts = lax.all_to_all(terms.reshape(N_OUTER, PART, BLK), OUTER, 0, 0, tiled=True)
    over_outer = call(
        sum_parts_kernel, shaped((PART, BLK), bf16), (parts,), nbytes=2 * 2**20, name="sum_outer"
    )
    weights, over_outer = lax.optimization_barrier((weights, over_outer))
    others = [swapped(over_outer, "y", n) for n in (1, 2, 3)]

    query_grad, sent, kept = call(
        backward_kernel,
        (shaped((PAIR, HALF), bf16), shaped((PAIR, HW), bf16), shaped((PAIR, HW), f32)),
        (at, weights, query_all, attended_grad, own, partner, before, crossed),
        scratch=(pltpu.VMEM((2 * PAIR, KVW), bf16), pltpu.VMEM((2 * PAIR, HW), f32)),
        flops=2 * PAIR * HALF * 4 * 3 * TOK,
        nbytes=6 * 2**20,
        name="backward",
    )

    slot_part = sum((p.astype(f32) for p in others), over_outer.astype(f32)).astype(bf16)
    slot_zl = swapped(slot_part, "zl")
    slot_c = swapped(slot_part, "c")
    slot_zl_c = swapped(slot_zl, "c")
    back = lax.ppermute(sent, SEQ, [(i + 2, i) for i in range(N_SEQ - 2)])

    new_statistics, update_rows = call(
        newton_kernel,
        (shaped((1, 2, ROWS, BLK), f32), shaped((NBLK, ROWS, BLK), bf16)),
        (at, slot_part, slot_zl, slot_c, slot_zl_c, stats_all, statistics),
        scratch=(
            pltpu.VMEM((BLK, BLK), bf16), pltpu.VMEM((BLK, BLK), f32), pltpu.VMEM((BLK, BLK), f32)
        ),
        flops=2 * BLK**3 * 5,
        nbytes=4 * 2**20,
        name="newton",
    )
    slots = lax.all_to_all(update_rows, REP, 0, 0, tiled=True)
    update = call(order_kernel, shaped((NBLK, ROWS, BLK), bf16), (owners, slots), name="order")

    mine, theirs = call(
        gather_grads_kernel,
        (shaped((TOK, 3 * HALF), bf16), shaped((TOK, 3 * HALF), bf16)),
        (at, query_grad, kept, back),
        name="gather_grads",
    )
    received = swapped(theirs, "c")
    query_out, key_out, value_out = call(
        whole_width_kernel,
        tuple(shaped((1, TOK, HW), bf16) for _ in range(3)),
        (at, mine, received),
        name="whole_width",
    )
    return query_out, key_out, value_out, new_statistics, update


def solution(mesh):
    split = Mesh(mesh.devices.reshape(2, 4, 2, 2, 4), ("zl", "y", "c", "zh", "x"))
    tokens = P(REP, SEQ, None)
    return jax.shard_map(
        local,
        mesh=split,
        in_specs=(
            tokens, tokens, tokens, tokens, P(REP, SEQ), P(), P(), P(REP, None, SEQ, None),
        ),
        out_specs=(tokens, tokens, tokens, P(REP, None, SEQ, None), P(None, SEQ, None)),
        check_vma=False,
    )
```

time: 345 us -> 130 us (0.38)
  matrix products: 84.2 us -> 0 us
  waiting for transfers between devices: 123 us -> 47.1 us
  blocking collectives: 55.1 us -> 12.7 us
  Pallas kernels: 0 us -> 18.3 us
  local copies, waits for them, and re-layouts: 25.7 us -> 7.84 us
  other arithmetic: 10.3 us -> 1.69 us
    reduce_scatter x2 -> x0, waiting for transfers between devices: 94.8 us -> none  [the longest x1 74.1 us: local(): lax.psum_scatter(partial_sum, 'rep', scatter_dimension=0, tiled=True)]
    dot_general x72 -> x0, matrix products: 84.2 us -> none  [the longest x17 25.6 us: contract_first(): lax.dot_general(left_mat, right_mat, (((0,), (0,)), ((), ())), preferred_...]
    all_gather x2 -> x0, blocking collectives: 55.1 us -> none  [the longest x1 34.4 us: local(): every_update = lax.all_gather(slot_updates, 'rep', axis=0, tiled=True)]
    all_to_all x0 -> x1, waiting for transfers between devices: none -> 32.4 us  [local(): lax.all_to_all(terms.reshape(N_OUTER, PART, BLK), OUTER, 0, 0, tiled=True)]
    all_gather x1, waiting for transfers between devices: 19.7 us -> 0.02 us  [local(): lax.all_gather(statistics[0].astype(bf16), SEQ, axis=0, tiled=False)]
    pallas_call x0 -> x9, Pallas kernels: none -> 18.3 us  [call(): pl.pallas_call(body, out_shape=outs, in_specs=specs, out_specs=jax.tree.m...]
    all_to_all x0 -> x1, blocking collectives: none -> 12.7 us  [local(): slots = lax.all_to_all(update_rows, REP, 0, 0, tiled=True)]
    ppermute x10 -> x13, starting transfers between devices: 27.4 us -> 15.4 us  [the longest x10 7.14 us: swapped(): return lax.ppermute(block, axis, [(i, i ^ mask) for i in range(n)])]
  transfers between devices with their start and end apart: 13 -> 15, of which waited for: 5 -> 5; matrix products, arithmetic and copies ran while one was open for 17% -> 1% of each run, Pallas kernels for 0% -> 10%
where the time goes in v1:
time: 130 us; the launch traced here: 128 us
  waiting for transfers between devices  47.1 us (36%)
  starting transfers between devices  25.8 us (20%)
  Pallas kernels  18.3 us (14%)
  between operations  14.3 us (11%)
  blocking collectives  12.7 us (10%)
  local copies, waits for them, and re-layouts  7.84 us (6%)
  other arithmetic  1.69 us (1%)
    all_to_all x1, waiting for transfers between devices, local(): lax.all_to_all(terms.reshape(N_OUTER, PART, BLK), OUTER, 0, 0, tiled=True)  32.4 us
    pallas_call x9, Pallas kernels, call(): pl.pallas_call(body, out_shape=outs, in_specs=specs, out_specs=jax.tree.m...  18.3 us
    all_to_all x1, blocking collectives, local(): slots = lax.all_to_all(update_rows, REP, 0, 0, tiled=True)  12.7 us
    all_to_all x1, starting transfers between devices, local(): lax.all_to_all(terms.reshape(N_OUTER, PART, BLK), OUTER, 0, 0, tiled=True)  10.4 us
    unnamed x34, local copies, waits for them, and re-layouts  7.84 us
    ppermute x10, starting transfers between devices, swapped(): return lax.ppermute(block, axis, [(i, i ^ mask) for i in range(n)])  7.14 us
    ppermute x1, waiting for transfers between devices, local(): back = lax.ppermute(sent, SEQ, [(i + 2, i) for i in range(N_SEQ - 2)])  6.66 us
    ppermute x1, waiting for transfers between devices, local(): lax.ppermute(other, SEQ, [(i, (i ^ 1) + 2) for i in range(N_SEQ - 2)])  4.16 us
  transfers between devices with their start and end apart: 15, of which 5 were waited for; matrix products, arithmetic and copies ran while one was open for 1% of the time, Pallas kernels for 10%

profile of v1, /device:TPU:0, one launch (start us, length us, event | category | flops | bytes accessed | tf_op | source)
XLA Modules:
  0.0 127.7 jit_solution(10408155464820038836)
XLA Ops:
  7.2 0.1 collective-permute-start.1
  7.3 0.5 collective-permute-start
  7.8 0.1 pad_add_fusion.at_ref
  7.8 0.9 copy-done.7
  8.8 0.9 copy-done.8
  9.7 0.7 copy-done.15
  10.4 0.6 pack.1
  11.0 0.2 collective-permute-start.2
  11.2 3.7 %collective-permute-start.3 = (bf16[128,1152]{1,0:T(8,128)(2,1)S(1)}, bf16[128,1152]{1,0:T(8,128)(2,1)S(1)}, u32[]{:S(2)}, u32[]{:S(2)}) collective-permute-start(bf16[128,1152]{1,0:T(8,128)(2,1)S(1)} %get-tuple-element.26.own_ref), channel_id=1, source_target_pairs={{0,16},{8,24},{16,32},{24,40},{32,48},{40,56},{48,64},{56,72},{64,... | collective-permute-start | bytes 884744 | tf_op jit(solution)/shard_map/ppermute | solution.py:281
  14.9 3.2 %collective-permute-start.4 = (bf16[128,1152]{1,0:T(8,128)(2,1)S(1)}, bf16[128,1152]{1,0:T(8,128)(2,1)S(1)}, u32[]{:S(2)}, u32[]{:S(2)}) collective-permute-start(bf16[128,1152]{1,0:T(8,128)(2,1)S(1)} %get-tuple-element.27), channel_id=1, source_target_pairs={{0,24},{8,16},{16,40},{24,32},{32,56},{40,48},{48,72},{56,64},{64,... | collective-permute-start | bytes 884744 | tf_op jit(solution)/shard_map/ppermute | solution.py:282
  18.2 0.0 collective-permute-done.query_other_ref
  18.2 0.0 collective-permute-done.1.grad_other_ref
  18.2 0.0 copy-start.1
  18.2 1.0 copy-done.1
  19.2 0.9 copy-done.6
  20.2 3.0 %grad_attended.1 = (bf16[256,512]{1,0:T(8,128)(2,1)S(1)}, bf16[256,512]{1,0:T(8,128)(2,1)S(1)}, bf16[256,2048]{1,0:T(8,128)(2,1)S(1)}) custom-call(s32[4]{0:T(128)S(1)} %pad_add_fusion.at_ref, bf16[128,1024]{1,0:T(8,128)(2,1)S(1)} %bitcast.13, bf16[128,1024]{1,0:T(8,128)(2,1)S(1)} %collective-permute-done.query_other_ref, bf16[128,2048]{1,0:T(8,128)(2,1)S(1)} %bitcast.11, ...), custom_call_target="tpu_custom_call" | custom-call | flops 536870912 | bytes 8388608 | tf_op jit(solution)/shard_map/grad_attended/pallas_call | solution.py:56
  23.2 0.0 copy-start.9
  23.2 0.7 copy-done.9
  23.9 0.0 collective-permute-done.2.other_ref
  23.9 0.0 collective-permute-done.3.before_ref
  23.9 0.0 copy-start.2
  23.9 4.2 %collective-permute-done.4.crossed_ref = bf16[128,1152]{1,0:T(8,128)(2,1)S(1)} collective-permute-done((bf16[128,1152]{1,0:T(8,128)(2,1)S(1)}, bf16[128,1152]{1,0:T(8,128)(2,1)S(1)}, u32[]{:S(2)}, u32[]{:S(2)}) %collective-permute-start.4) | collective-permute-done | bytes 294944 | tf_op jit(solution)/shard_map/ppermute | solution.py:282
  28.1 0.0 copy-done.14
  28.1 4.1 %forward.1 = (bf16[2,8,128,512]{3,2,1,0:T(8,128)(2,1)S(1)}, bf16[4,2,128,384]{3,2,1,0:T(8,128)(2,1)S(1)}) custom-call(s32[4]{0:T(128)S(1)} %pad_add_fusion.at_ref, s32[8]{0:T(128)S(1)} %copy-done.14, bf16[256,512]{1,0:T(8,128)(2,1)S(1)} %get-tuple-element.24.query_ref, bf16[256,2048]{1,0:T(8,128)(2,1)S(1)} %get-tuple-element.25.grad_ref, ...), custom_call_target="tpu_custom_call" | custom-call | flops 738197504 | bytes 6291456 | tf_op jit(solution)/shard_map/forward/pallas_call | solution.py:56
  32.1 0.0 copy-done.2
  32.1 0.0 copy-start
  32.1 1.3 %copy-done = bf16[2,8,128,512]{3,2,1,0:T(8,128)(2,1)} copy-done((bf16[2,8,128,512]{3,2,1,0:T(8,128)(2,1)}, bf16[2,8,128,512]{3,2,1,0:T(8,128)(2,1)S(1)}, u32[]{:S(2)}) %copy-start) | copy-done | bytes 2097176
  33.5 0.0 copy-done.4
  33.5 0.0 copy-done.11
  33.5 10.4 %all-to-all-start = ((bf16[16,128,512]{2,1,0:T(8,128)(2,1)}), bf16[16,128,512]{2,1,0:T(8,128)(2,1)S(1)}, u32[]{:S(2)}, u32[]{:S(2)}) async-start(bf16[16,128,512]{2,1,0:T(8,128)(2,1)} %bitcast.9), calls=%async_computation | async-start | bytes 4194304 | tf_op jit(solution)/shard_map/all_to_all | solution.py:304
  43.9 0.0 all-gather.2.cloned.1.call-start
  44.0 1.5 %convert_element_type.24 = bf16[1,2,32,512]{3,2,1,0:T(8,128)(2,1)} convert(f32[1,2,32,512]{3,2,1,0:T(8,128)} %stat_rows_ref.1) | non-fusion elementwise | flops 32768 | bytes 196608 | tf_op jit(solution)/shard_map/convert_element_type | solution.py:273
  45.5 0.0 all-gather.2.cloned.1.call-update
  45.5 32.4 %all-to-all-done.parts_ref = bf16[16,128,512]{2,1,0:T(8,128)(2,1)S(1)} async-done(((bf16[16,128,512]{2,1,0:T(8,128)(2,1)}), bf16[16,128,512]{2,1,0:T(8,128)(2,1)S(1)}, u32[]{:S(2)}, u32[]{:S(2)}) %all-to-all-start) | async-done | bytes 2097184 | tf_op jit(solution)/shard_map/all_to_all | solution.py:304
  77.9 0.3 sum_outer.1
  78.2 1.0 collective-permute-start.9
  79.1 0.6 collective-permute-start.8
  79.7 2.6 %collective-permute-start.7 = (bf16[128,512]{1,0:T(8,128)(2,1)S(1)}, bf16[128,512]{1,0:T(8,128)(2,1)S(1)}, u32[]{:S(2)}, u32[]{:S(2)}) collective-permute-start(bf16[128,512]{1,0:T(8,128)(2,1)S(1)} %sum_outer.1), channel_id=1, source_target_pairs={{0,16},{16,0},{32,48},{48,32},{1,17},{17,1},{33,49},{49,33},{2,18}... | collective-permute-start | bytes 393224 | tf_op jit(solution)/shard_map/ppermute | solution.py:264
  82.4 0.0 copy-done.3
  82.4 0.0 copy-start.13
  82.4 3.6 %backward.1 = (bf16[256,512]{1,0:T(8,128)(2,1)S(1)}, bf16[256,1024]{1,0:T(8,128)(2,1)S(1)}, f32[256,1024]{1,0:T(8,128)S(1)}) custom-call(s32[4]{0:T(128)S(1)} %pad_add_fusion.at_ref, bf16[4,2,128,384]{3,2,1,0:T(8,128)(2,1)S(1)} %get-tuple-element.30.weights_ref, bf16[256,512]{1,0:T(8,128)(2,1)S(1)} %copy-done.12, bf16[256,512]{1,0:T(8,128)(2,1)S(1)} %copy-done.10, ...), custom_call_target="tpu_custom_call" | custom-call | flops 402653184 | bytes 6291456 | tf_op jit(solution)/shard_map/backward/pallas_call | solution.py:56
  86.0 1.3 %collective-permute-start.5 = (bf16[256,1024]{1,0:T(8,128)(2,1)S(1)}, bf16[256,1024]{1,0:T(8,128)(2,1)S(1)}, u32[]{:S(2)}, u32[]{:S(2)}) collective-permute-start(bf16[256,1024]{1,0:T(8,128)(2,1)S(1)} %get-tuple-element.34), channel_id=1, source_target_pairs={{16,0},{24,8},{32,16},{40,24},{48,32},{56,40},{64,48},{72,56},{80,... | collective-permute-start | bytes 1572872 | tf_op jit(solution)/shard_map/ppermute | solution.py:325
  87.3 0.0 collective-permute-done.9
  87.3 0.0 collective-permute-done.8
  87.3 0.9 collective-permute-done.7
  88.2 0.1 add_convert_fusion.grad_ref
  88.3 2.1 %collective-permute-start.10 = (bf16[128,512]{1,0:T(8,128)(2,1)S(1)}, bf16[128,512]{1,0:T(8,128)(2,1)S(1)}, u32[]{:S(2)}, u32[]{:S(2)}) collective-permute-start(bf16[128,512]{1,0:T(8,128)(2,1)S(1)} %add_convert_fusion.grad_ref), channel_id=1, source_target_pairs={{0,64},{64,0},{1,65},{65,1},{2,66},{66,2},{3,67},{67,3},{4,68},{68... | collective-permute-start | bytes 393224 | tf_op jit(solution)/shard_map/ppermute | solution.py:264
  90.4 0.0 collective-permute-start.11
  90.4 2.9 %collective-permute-done.10.grad_zl_ref = bf16[128,512]{1,0:T(8,128)(2,1)S(1)} collective-permute-done((bf16[128,512]{1,0:T(8,128)(2,1)S(1)}, bf16[128,512]{1,0:T(8,128)(2,1)S(1)}, u32[]{:S(2)}, u32[]{:S(2)}) %collective-permute-start.10) | collective-permute-done | bytes 131104 | tf_op jit(solution)/shard_map/ppermute | solution.py:264
  93.4 0.0 collective-permute-start.12
  93.4 6.7 %collective-permute-done.5.back_ref = bf16[256,1024]{1,0:T(8,128)(2,1)S(1)} collective-permute-done((bf16[256,1024]{1,0:T(8,128)(2,1)S(1)}, bf16[256,1024]{1,0:T(8,128)(2,1)S(1)}, u32[]{:S(2)}, u32[]{:S(2)}) %collective-permute-start.5) | collective-permute-done | bytes 524320 | tf_op jit(solution)/shard_map/ppermute | solution.py:325
  100.0 0.6 gather_grads.1
  100.7 0.1 collective-permute-start.6
  100.8 0.0 all-gather.2.cloned.1.call-done.stats_ref
  100.8 0.0 collective-permute-done.11.grad_c_ref
  100.8 0.0 collective-permute-done.12.grad_zl_c_ref
  100.8 0.0 copy-done.13
  100.8 0.0 copy-start.16
  100.8 1.2 copy-done.16
  102.1 3.3 %newton.1 = (f32[1,2,32,512]{3,2,1,0:T(8,128)}, bf16[8,32,512]{2,1,0:T(8,128)(2,1)S(1)}) custom-call(s32[4]{0:T(128)S(1)} %pad_add_fusion.at_ref, bf16[128,512]{1,0:T(8,128)(2,1)S(1)} %add_convert_fusion.grad_ref, bf16[128,512]{1,0:T(8,128)(2,1)S(1)} %collective-permute-done.10.grad_zl_ref, bf16[128,512]{1,0:T(8,128)(2,1)S(1)} %collective-permute-done.11.grad_c_ref, ...), custom_call_target="tpu_custom_call" | custom-call | flops 1342177280 | bytes 4194304 | tf_op jit(solution)/shard_map/newton/pallas_call | solution.py:56
  105.4 12.7 %all_to_all.10.slots_ref = bf16[8,32,512]{2,1,0:T(8,128)(2,1)S(1)} all-to-all(bf16[8,32,512]{2,1,0:T(8,128)(2,1)S(1)} %get-tuple-element.42), channel_id=1, replica_groups=mesh['zl'=2,'y'=4,'c'=2,'zh'=2,'x'=4] {'zh','x'}, dimensions={0} | all-to-all | bytes 524288 | tf_op jit(solution)/shard_map/all_to_all | solution.py:338
  118.1 1.3 order.1
  119.4 0.0 collective-permute-done.6.other_ref
  119.4 1.5 %whole_width.1 = (bf16[1,128,1024]{2,1,0:T(8,128)(2,1)}, bf16[1,128,1024]{2,1,0:T(8,128)(2,1)}, bf16[1,128,1024]{2,1,0:T(8,128)(2,1)}) custom-call(s32[4]{0:T(128)S(1)} %pad_add_fusion.at_ref, bf16[128,1536]{1,0:T(8,128)(2,1)S(1)} %get-tuple-element.35.mine_ref, bf16[128,1536]{1,0:T(8,128)(2,1)S(1)} %collective-permute-done.6.other_ref), custom_call_target="tpu_custom_call" | custom-call | tf_op jit(solution)/shard_map/whole_width/pallas_call | solution.py:56
  (14 shorter events, 0.0 us)
Async XLA Ops:
  7.2 11.0 %collective-permute-start.1 = (bf16[128,2048]{1,0:T(8,128)(2,1)}, bf16[128,2048]{1,0:T(8,128)(2,1)S(1)}, u32[]{:S(2)}, u32[]{:S(2)}) collective-permute-start(bf16[128,2048]{1,0:T(8,128)(2,1)} %bitcast.10), channel_id=1, source_target_pairs={{0,8},{8,0},{1,9},{9,1},{2,10},{10,2},{3,11},{11,3},{4,12},{12,4},... | collective-permute-start | bytes 1572872 | tf_op jit(solution)/shard_map/ppermute | solution.py:264
  7.3 10.9 %collective-permute-start = (bf16[128,1024]{1,0:T(8,128)(2,1)}, bf16[128,1024]{1,0:T(8,128)(2,1)S(1)}, u32[]{:S(2)}, u32[]{:S(2)}) collective-permute-start(bf16[128,1024]{1,0:T(8,128)(2,1)} %bitcast.12), channel_id=1, source_target_pairs={{0,8},{8,0},{1,9},{9,1},{2,10},{10,2},{3,11},{11,3},{4,12},{12,4},... | collective-permute-start | bytes 786440 | tf_op jit(solution)/shard_map/ppermute | solution.py:264
  7.8 1.0 copy-start.7
  8.8 0.9 copy-start.8
  9.7 0.7 copy-start.15
  11.0 12.9 %collective-permute-start.2 = (bf16[128,1152]{1,0:T(8,128)(2,1)S(1)}, bf16[128,1152]{1,0:T(8,128)(2,1)S(1)}, u32[]{:S(2)}, u32[]{:S(2)}) collective-permute-start(bf16[128,1152]{1,0:T(8,128)(2,1)S(1)} %get-tuple-element.27), channel_id=1, source_target_pairs={{0,8},{8,0},{1,9},{9,1},{2,10},{10,2},{3,11},{11,3},{4,12},{12,4},... | collective-permute-start | bytes 884744 | tf_op jit(solution)/shard_map/ppermute | solution.py:264
  11.2 16.9 %copy-start.14 = (s32[8]{0:T(128)S(1)}, s32[8]{0:T(128)}, u32[]{:S(2)}) copy-start(s32[8]{0:T(128)} %owner_ref.3) | copy-start | bytes 100
  11.2 12.7 %collective-permute-start.3 = (bf16[128,1152]{1,0:T(8,128)(2,1)S(1)}, bf16[128,1152]{1,0:T(8,128)(2,1)S(1)}, u32[]{:S(2)}, u32[]{:S(2)}) collective-permute-start(bf16[128,1152]{1,0:T(8,128)(2,1)S(1)} %get-tuple-element.26.own_ref), channel_id=1, source_target_pairs={{0,16},{8,24},{16,32},{24,40},{32,48},{40,56},{48,64},{56,72},{64,... | collective-permute-start | bytes 884744 | tf_op jit(solution)/shard_map/ppermute | solution.py:281
  14.9 13.1 %collective-permute-start.4 = (bf16[128,1152]{1,0:T(8,128)(2,1)S(1)}, bf16[128,1152]{1,0:T(8,128)(2,1)S(1)}, u32[]{:S(2)}, u32[]{:S(2)}) collective-permute-start(bf16[128,1152]{1,0:T(8,128)(2,1)S(1)} %get-tuple-element.27), channel_id=1, source_target_pairs={{0,24},{8,16},{16,40},{24,32},{32,56},{40,48},{48,72},{56,64},{64,... | collective-permute-start | bytes 884744 | tf_op jit(solution)/shard_map/ppermute | solution.py:282
  18.2 1.0 copy-start.1
  19.2 0.9 copy-start.6
  23.2 0.7 copy-start.9
  23.9 9.6 %copy-start.11 = (bf16[256,512]{1,0:T(8,128)(2,1)}, bf16[256,512]{1,0:T(8,128)(2,1)S(1)}, u32[]{:S(2)}) copy-start(bf16[256,512]{1,0:T(8,128)(2,1)S(1)} %get-tuple-element.24.query_ref) | copy-start | bytes 786436
  23.9 8.2 %copy-start.2 = (bf16[128,1152]{1,0:T(8,128)(2,1)}, bf16[128,1152]{1,0:T(8,128)(2,1)S(1)}, u32[]{:S(2)}) copy-start(bf16[128,1152]{1,0:T(8,128)(2,1)S(1)} %collective-permute-done.3.before_ref) | copy-start | bytes 884740
  28.1 5.4 %copy-start.4 = (bf16[128,1152]{1,0:T(8,128)(2,1)}, bf16[128,1152]{1,0:T(8,128)(2,1)S(1)}, u32[]{:S(2)}) copy-start(bf16[128,1152]{1,0:T(8,128)(2,1)S(1)} %collective-permute-done.4.crossed_ref) | copy-start | bytes 884740
  32.1 1.4 %copy-start = (bf16[2,8,128,512]{3,2,1,0:T(8,128)(2,1)}, bf16[2,8,128,512]{3,2,1,0:T(8,128)(2,1)S(1)}, u32[]{:S(2)}) copy-start(bf16[2,8,128,512]{3,2,1,0:T(8,128)(2,1)S(1)} %get-tuple-element.29) | copy-start | bytes 6291460
  33.5 44.4 %all-to-all-start = ((bf16[16,128,512]{2,1,0:T(8,128)(2,1)}), bf16[16,128,512]{2,1,0:T(8,128)(2,1)S(1)}, u32[]{:S(2)}, u32[]{:S(2)}) async-start(bf16[16,128,512]{2,1,0:T(8,128)(2,1)} %bitcast.9), calls=%async_computation | async-start | bytes 4194304 | tf_op jit(solution)/shard_map/all_to_all | solution.py:304
  43.9 56.9 %all-gather.2.cloned.1.call-start = ((), (), s32[]{:S(2)}) async-start(), calls=%async_computation.2 | async-start | bytes 1114112 | tf_op jit(solution)/shard_map/all_gather | solution.py:273
  77.9 4.5 %copy-start.3 = (bf16[128,1152]{1,0:T(8,128)(2,1)S(1)}, bf16[128,1152]{1,0:T(8,128)(2,1)}, u32[]{:S(2)}) copy-start(bf16[128,1152]{1,0:T(8,128)(2,1)} %copy-done.2) | copy-start | bytes 884740
  77.9 4.5 %copy-start.5 = (bf16[128,1152]{1,0:T(8,128)(2,1)S(1)}, bf16[128,1152]{1,0:T(8,128)(2,1)}, u32[]{:S(2)}) copy-start(bf16[128,1152]{1,0:T(8,128)(2,1)} %copy-done.4) | copy-start | bytes 884740
  77.9 4.5 %copy-start.10 = (bf16[256,512]{1,0:T(8,128)(2,1)S(1)}, bf16[256,512]{1,0:T(8,128)(2,1)}, u32[]{:S(2)}) copy-start(bf16[256,512]{1,0:T(8,128)(2,1)} %copy-done.9) | copy-start | bytes 786436
  77.9 4.5 %copy-start.12 = (bf16[256,512]{1,0:T(8,128)(2,1)S(1)}, bf16[256,512]{1,0:T(8,128)(2,1)}, u32[]{:S(2)}) copy-start(bf16[256,512]{1,0:T(8,128)(2,1)} %copy-done.11) | copy-start | bytes 786436
  78.2 9.1 %collective-permute-start.9 = (bf16[128,512]{1,0:T(8,128)(2,1)S(1)}, bf16[128,512]{1,0:T(8,128)(2,1)S(1)}, u32[]{:S(2)}, u32[]{:S(2)}) collective-permute-start(bf16[128,512]{1,0:T(8,128)(2,1)S(1)} %sum_outer.1), channel_id=1, source_target_pairs={{0,48},{16,32},{32,16},{48,0},{1,49},{17,33},{33,17},{49,1},{2,50}... | collective-permute-start | bytes 393224 | tf_op jit(solution)/shard_map/ppermute | solution.py:264
  79.1 8.2 %collective-permute-start.8 = (bf16[128,512]{1,0:T(8,128)(2,1)S(1)}, bf16[128,512]{1,0:T(8,128)(2,1)S(1)}, u32[]{:S(2)}, u32[]{:S(2)}) collective-permute-start(bf16[128,512]{1,0:T(8,128)(2,1)S(1)} %sum_outer.1), channel_id=1, source_target_pairs={{0,32},{16,48},{32,0},{48,16},{1,33},{17,49},{33,1},{49,17},{2,34}... | collective-permute-start | bytes 393224 | tf_op jit(solution)/shard_map/ppermute | solution.py:264
  79.7 8.5 %collective-permute-start.7 = (bf16[128,512]{1,0:T(8,128)(2,1)S(1)}, bf16[128,512]{1,0:T(8,128)(2,1)S(1)}, u32[]{:S(2)}, u32[]{:S(2)}) collective-permute-start(bf16[128,512]{1,0:T(8,128)(2,1)S(1)} %sum_outer.1), channel_id=1, source_target_pairs={{0,16},{16,0},{32,48},{48,32},{1,17},{17,1},{33,49},{49,33},{2,18}... | collective-permute-start | bytes 393224 | tf_op jit(solution)/shard_map/ppermute | solution.py:264
  82.4 18.5 %copy-start.13 = (f32[1,2,32,512]{3,2,1,0:T(8,128)S(1)}, f32[1,2,32,512]{3,2,1,0:T(8,128)}, u32[]{:S(2)}) copy-start(f32[1,2,32,512]{3,2,1,0:T(8,128)} %stat_rows_ref.1) | copy-start | bytes 393220
  86.0 14.1 %collective-permute-start.5 = (bf16[256,1024]{1,0:T(8,128)(2,1)S(1)}, bf16[256,1024]{1,0:T(8,128)(2,1)S(1)}, u32[]{:S(2)}, u32[]{:S(2)}) collective-permute-start(bf16[256,1024]{1,0:T(8,128)(2,1)S(1)} %get-tuple-element.34), channel_id=1, source_target_pairs={{16,0},{24,8},{32,16},{40,24},{48,32},{56,40},{64,48},{72,56},{80,... | collective-permute-start | bytes 1572872 | tf_op jit(solution)/shard_map/ppermute | solution.py:325
  88.3 5.1 %collective-permute-start.10 = (bf16[128,512]{1,0:T(8,128)(2,1)S(1)}, bf16[128,512]{1,0:T(8,128)(2,1)S(1)}, u32[]{:S(2)}, u32[]{:S(2)}) collective-permute-start(bf16[128,512]{1,0:T(8,128)(2,1)S(1)} %add_convert_fusion.grad_ref), channel_id=1, source_target_pairs={{0,64},{64,0},{1,65},{65,1},{2,66},{66,2},{3,67},{67,3},{4,68},{68... | collective-permute-start | bytes 393224 | tf_op jit(solution)/shard_map/ppermute | solution.py:264
  90.4 10.4 %collective-permute-start.11 = (bf16[128,512]{1,0:T(8,128)(2,1)S(1)}, bf16[128,512]{1,0:T(8,128)(2,1)S(1)}, u32[]{:S(2)}, u32[]{:S(2)}) collective-permute-start(bf16[128,512]{1,0:T(8,128)(2,1)S(1)} %add_convert_fusion.grad_ref), channel_id=1, source_target_pairs={{0,8},{8,0},{1,9},{9,1},{2,10},{10,2},{3,11},{11,3},{4,12},{12,4},... | collective-permute-start | bytes 393224 | tf_op jit(solution)/shard_map/ppermute | solution.py:264
  93.4 7.5 %collective-permute-start.12 = (bf16[128,512]{1,0:T(8,128)(2,1)S(1)}, bf16[128,512]{1,0:T(8,128)(2,1)S(1)}, u32[]{:S(2)}, u32[]{:S(2)}) collective-permute-start(bf16[128,512]{1,0:T(8,128)(2,1)S(1)} %collective-permute-done.10.grad_zl_ref), channel_id=1, source_target_pairs={{0,8},{8,0},{1,9},{9,1},{2,10},{10,2},{3,11},{11,3},{4,12},{12,4},... | collective-permute-start | bytes 393224 | tf_op jit(solution)/shard_map/ppermute | solution.py:264
  100.7 18.7 %collective-permute-start.6 = (bf16[128,1536]{1,0:T(8,128)(2,1)S(1)}, bf16[128,1536]{1,0:T(8,128)(2,1)S(1)}, u32[]{:S(2)}, u32[]{:S(2)}) collective-permute-start(bf16[128,1536]{1,0:T(8,128)(2,1)S(1)} %get-tuple-element.36), channel_id=1, source_target_pairs={{0,8},{8,0},{1,9},{9,1},{2,10},{10,2},{3,11},{11,3},{4,12},{12,4},... | collective-permute-start | bytes 1179656 | tf_op jit(solution)/shard_map/ppermute | solution.py:264
  100.8 1.2 copy-start.16
Sparse Core Ops, SparseCore 0:
  47.0 41.6 all-gather.1
